TPU v7x, 256 devices: a whole 4x4x8 slice. The times are simulated.
256 devices in a mesh: row: 16 (over x_hi, y, core), col: 16 (over z, x_lo).
Axes of the slice: x: 4 (x_hi: 2, x_lo: 2; x = x_hi * 2 + x_lo), y: 4, z: 8, core: 2. Of those that a mesh axis runs over, the one named last changes fastest.
Arguments:
- coords: float32 [2, 131072], P(None, 'row'), may hold values from 0 to 1
- order: int32 [131072], replicated, may hold values from 0 to 131071, as said below
- panel_index: int32 [1], replicated, may hold values from 0 to 253
- trailing: float32 [16, 16, 1024, 512], P(None, 'row', 'col'), may hold values from -6 to 6
Outputs:
- panel_factor: float32 [16, 16, 512, 512], P(None, 'row', 'col')
- new_trailing: float32 [16, 16, 1024, 512], P(None, 'row', 'col')
Inputs may be any that keep to these rules, and one draw needn't show every extreme that they name: order is a permutation of the matrix indices that maps index m to a location of the same owner range: m // 8192 == order[m] // 8192.
All inputs are finite; a program needn't handle non-finite values.
Results may differ from a plain program's by a relative error of at most 0.0003.
Values sent between devices are 32-bit elements; how exact they have to be, the bound alone decides.
No kernel may reach another device: no remote copies, remote signals or barrier semaphores. Data moves between devices by JAX's collectives and lax.ppermute only.
A program may use at most 128 MiB of HBM per device.

v0:
```python
import math

import jax
import jax.numpy as jnp
from jax import lax
from jax.sharding import PartitionSpec as P

B = 512


ROOT_THREE = math.sqrt(3.0)
LENGTH = 0.05
NUGGET = 1.0


def matern(row_x, row_y, col_x, col_y):
    diff_x = row_x[..., :, None] - col_x
    diff_y = row_y[..., :, None] - col_y
    scaled = ROOT_THREE / LENGTH * jnp.sqrt(diff_x * diff_x + diff_y * diff_y)
    return (1.0 + scaled) * jnp.exp(-scaled)


def right_solve(factor, rows):
    return lax.linalg.triangular_solve(factor, rows, left_side=False, lower=True, transpose_a=True)


def on_device(coords, order, panel_index, trailing):
    owners = lax.axis_size("row")
    columns = lax.axis_size("col")
    here_row = lax.axis_index("row")
    here_col = lax.axis_index("col")
    local_blocks = trailing.shape[0]
    span = trailing.shape[2]
    share = B // columns
    owned = local_blocks * B
    block_k = panel_index[0]
    start = block_k * B
    mine = lax.dynamic_slice_in_dim(order, here_row * owned, owned) - here_row * owned
    located = jnp.take(coords, mine, axis=1)
    wanted = start + jnp.arange(3 * B, dtype=jnp.int32) - here_row * owned
    inside = ((wanted >= 0) & (wanted < owned)).astype(jnp.float32)
    picked = jnp.take(located, jnp.clip(wanted, 0, owned - 1), axis=1) * inside
    pivot = lax.psum(picked, "row")
    pivot_x = pivot[0, :B]
    pivot_y = pivot[1, :B]
    pivot_ids = start + jnp.arange(B, dtype=jnp.int32)
    diag = matern(pivot_x, pivot_y, pivot_x, pivot_y) + NUGGET * jnp.eye(B, dtype=jnp.float32)
    factor = jnp.linalg.cholesky(diag)
    far = lax.dynamic_slice_in_dim(pivot, B + here_col * span, span, 1)
    far_cov = matern(far[0], far[1], pivot_x, pivot_y)
    far_factor = right_solve(factor, far_cov)
    cyclic = jnp.arange(local_blocks, dtype=jnp.int32) * owners + here_row
    rows_in = here_col * share + jnp.arange(share, dtype=jnp.int32)
    own_blocks = here_row * local_blocks + jnp.arange(local_blocks, dtype=jnp.int32)
    part_xy = lax.dynamic_slice_in_dim(
        located.reshape(2, local_blocks, B), here_col * share, share, 2
    )
    row_ids = own_blocks[:, None] * B + rows_in[None, :]
    nugget = NUGGET * (row_ids[:, :, None] == pivot_ids).astype(jnp.float32)
    made = matern(part_xy[0], part_xy[1], pivot_x, pivot_y) + nugget
    grouped = made.reshape(local_blocks // owners, owners, share, B)
    cov = lax.all_to_all(grouped, "row", split_axis=1, concat_axis=0, tiled=True).reshape(
        local_blocks, share, B
    )
    solved = right_solve(factor, cov.reshape(-1, B)).reshape(local_blocks, share, B)
    panel_share = jnp.where((cyclic >= block_k)[:, None, None], solved, jnp.zeros_like(solved))
    updates = jnp.einsum(
        "wb,lsb->lws",
        far_factor,
        lax.all_gather(panel_share, "col", axis=1, tiled=True),
        precision=lax.Precision.HIGHEST,
    )
    updates = jnp.where((cyclic > block_k)[:, None, None], updates, jnp.zeros_like(updates))
    new_trailing = trailing - updates[:, None]
    return (panel_share[:, None], new_trailing)


def solution(mesh):
    placed = (P(None, "row"), P(), P(), P(None, "row", "col", None))
    return jax.shard_map(
        on_device,
        mesh=mesh,
        in_specs=placed,
        out_specs=(P(None, "row", "col", None), P(None, "row", "col", None)),
        check_vma=False,
    )
```

profile of v0, /device:TPU:1, one launch (start us, length us, event | category | flops | bytes accessed | tf_op | source)
XLA Modules:
  0.0 673.1 jit_solution(18203027445314878240)
XLA Ops:
  7.9 0.8 compare_and_fusion
  8.7 0.8 fusion.50
  9.5 3.4 copy.18
  12.9 29.9 %gather_fusion = f32[8192,2]{1,0:T(8,128)} fusion(f32[2,8192]{0,1:T(8,128)} %copy.18, s32[8192]{0:T(1024)S(1)} %fusion.50), kind=kCustom, calls=%fused_computation | custom fusion | bytes 163840 | tf_op jit(solution)/shard_map/jit(_take)/gather | solution.py:39
  42.8 7.5 %bitcast_select_fusion = f32[2,8192]{0,1:T(8,128)} fusion(f32[8192,2]{1,0:T(8,128)} %gather_fusion, pred[8192]{0:T(1024)(128)(4,1)S(1)} %compare_and_fusion), kind=kLoop, calls=%fused_computation.4 | loop fusion | flops 16384 | bytes 139264 | tf_op jit(solution)/shard_map/jit(_take)/select_n | solution.py:39
  50.3 1.0 constant_dynamic-slice_fusion.2
  51.5 4.8 gather_fusion.1
  56.3 1.1 multiply_bitcast_fusion
  57.4 73.1 %psum.7 = f32[2,1536]{0,1:T(8,128)S(1)} all-reduce(f32[2,1536]{0,1:T(8,128)S(1)} %multiply_bitcast_fusion), channel_id=1, replica_groups=mesh['row'=16,'col'=16] {'row'}, use_global_device_ids=true, to_apply=%region_0.1 | all-reduce | flops 3072 | bytes 24576 | tf_op jit(solution)/shard_map/psum | solution.py:43
  130.8 1.8 convert_add_fusion
  132.6 9.6 %all-to-all-start = ((f32[1,16,32,512]{3,2,0,1:T(8,128)}), f32[1,16,32,512]{3,2,0,1:T(8,128)S(1)}, u32[]{:S(2)}, u32[]{:S(2)}) async-start(f32[1,16,32,512]{3,2,0,1:T(8,128)} %convert_add_fusion), calls=%async_computation | async-start | bytes 2097152 | tf_op jit(solution)/shard_map/all_to_all | solution.py:62
  142.2 0.6 all-gather.2.cloned.1.call-start
  142.8 1.4 add_multiply_fusion
  144.3 1.0 copy-done.1
  145.2 11.7 %cholesky.104 = f32[128,128]{1,0:T(8,128)S(1)} custom-call(f32[128,128]{1,0:T(8,128)S(1)} %cholesky.266), custom_call_target="Cholesky" | custom-call | tf_op jit(solution)/shard_map/jit(cholesky)/cholesky | solution.py:48
  157.0 0.7 compare_reduce_fusion.3
  157.6 9.8 %custom-call.32 = f32[1,128,128]{1,2,0:T(8,128)S(1)} custom-call(f32[1,128,128]{2,1,0:T(8,128)S(1)} %get-tuple-element.39), custom_call_target="InvertDiagBlocksLowerTriangular" | custom-call | tf_op jit(solution)/shard_map/jit(cholesky)/cholesky | solution.py:48
  167.6 1.2 constant_dynamic-update-slice_fusion.1
  168.8 1.3 convolution_subtract_fusion.3
  170.1 11.7 %cholesky.217 = f32[128,128]{1,0:T(8,128)S(1)} custom-call(f32[128,128]{1,0:T(8,128)S(1)} %cholesky.270), custom_call_target="Cholesky" | custom-call | tf_op jit(solution)/shard_map/jit(cholesky)/cholesky | solution.py:48
  181.9 0.6 compare_reduce_fusion.2
  182.5 10.0 %custom-call.33 = f32[1,128,128]{1,2,0:T(8,128)S(1)} custom-call(f32[1,128,128]{2,1,0:T(8,128)S(1)} %get-tuple-element.36), custom_call_target="InvertDiagBlocksLowerTriangular" | custom-call | tf_op jit(solution)/shard_map/jit(cholesky)/cholesky | solution.py:48
  192.7 1.3 convolution_subtract_fusion.4
  194.0 11.7 %cholesky.238 = f32[128,128]{1,0:T(8,128)S(1)} custom-call(f32[128,128]{1,0:T(8,128)S(1)} %cholesky.275), custom_call_target="Cholesky" | custom-call | tf_op jit(solution)/shard_map/jit(cholesky)/cholesky | solution.py:48
  205.7 0.7 compare_reduce_fusion.1
  206.5 9.8 %custom-call.34 = f32[1,128,128]{1,2,0:T(8,128)S(1)} custom-call(f32[1,128,128]{2,1,0:T(8,128)S(1)} %get-tuple-element.33), custom_call_target="InvertDiagBlocksLowerTriangular" | custom-call | tf_op jit(solution)/shard_map/jit(cholesky)/cholesky | solution.py:48
  216.5 1.2 convolution_subtract_fusion.5
  217.7 11.9 %cholesky.255 = f32[128,128]{1,0:T(8,128)S(1)} custom-call(f32[128,128]{1,0:T(8,128)S(1)} %convolution_subtract_fusion.5), custom_call_target="Cholesky" | custom-call | tf_op jit(solution)/shard_map/jit(cholesky)/cholesky | solution.py:48
  229.7 0.6 compare_reduce_fusion
  233.0 10.4 %while.1 = (s32[]{:T(128)}, f32[512,512]{1,0:T(8,128)S(1)}, s32[4,2]{0,1:T(2,128)S(1)}, f32[4,128,128]{2,1,0:T(8,128)}, s32[]{:T(128)}) while((s32[]{:T(128)}, f32[512,512]{1,0:T(8,128)S(1)}, s32[4,2]{0,1:T(2,128)S(1)}, f32[4,128,128]{2,1,0:T(8,128)}, s32[]{:T(128)}) %tuple.37), condition=%wide.while_cond, body=%wide.while_body.sunk | while | flops 2 | bytes 132205 | solution.py:24
  233.1 0.5 fusion.78
  233.6 2.0 bitcast_dynamic-update-slice_fusion.2
  235.7 0.5 fusion.78
  236.2 2.0 bitcast_dynamic-update-slice_fusion.2
  238.3 0.5 fusion.78
  238.8 2.0 bitcast_dynamic-update-slice_fusion.2
  240.9 0.5 fusion.78
  241.4 2.0 bitcast_dynamic-update-slice_fusion.2
  243.4 40.1 %custom-call.35 = f32[4,128,128]{1,2,0:T(8,128)S(1)} custom-call(f32[4,128,128]{2,1,0:T(8,128)} %get-tuple-element.9), custom_call_target="InvertDiagBlocksLowerTriangular" | custom-call | tf_op jit(solution)/shard_map/triangular_solve | solution.py:24
  284.0 0.6 convolution_subtract_fusion.1
  285.0 1.0 convolution_subtract_fusion
  286.0 0.4 fusion.44
  286.4 1.5 convolution_subtract_fusion.2
  288.7 1.1 broadcast_select_fusion
  289.9 1.0 dynamic-slice_reduce_fusion.1
  292.7 1.1 select_bitcast_fusion
  293.8 349.8 %all-gather.2.cloned.1.call-done = f32[16,512,512]{2,1,0:T(8,128)} async-done(((f32[16,32,512]{2,1,0:T(8,128)}), f32[16,512,512]{2,1,0:T(8,128)}) %all-gather.2.cloned.1.call-update) | async-done | bytes 16777232 | tf_op jit(solution)/shard_map/all_gather | solution.py:70
  643.7 22.3 %fusion = f32[16,1,64,512]{3,2,1,0:T(8,128)} fusion(f32[16,1,64,512]{3,2,1,0:T(8,128)} %param.7, f32[16,512,512]{2,1,0:T(8,128)} %all-gather.2.cloned.1.call-done, pred[16]{0:T(512)(128)(4,1)S(1)} %fusion.59, f32[64,128]{1,0:T(8,128)S(1)} %fusion.45, f32[64,128]{1,0:T(8,128)S(1)} %fusion.43, f32[64,128]{1,0:T(8,128)S(1)} %fusion.41, f32[64,128]{1,0:T(8,128)S(1)} %fusion.40), kind=kOutput, calls=%fused_computation.6 | convolution fusion | flops 3222372352 | bytes 21102608 | tf_op jit(solution)/shard_map/wb,lsb->lws/dot_general | solution.py:67
  (51 shorter events, 5.3 us)
Async XLA Ops:
  130.4 27.2 %copy-start = (f32[2,1536]{0,1:T(8,128)}, f32[2,1536]{0,1:T(8,128)S(1)}, u32[]{:S(2)}) copy-start(f32[2,1536]{0,1:T(8,128)S(1)} %psum.7) | copy-start | bytes 36868
  132.6 151.0 %all-to-all-start = ((f32[1,16,32,512]{3,2,0,1:T(8,128)}), f32[1,16,32,512]{3,2,0,1:T(8,128)S(1)}, u32[]{:S(2)}, u32[]{:S(2)}) async-start(f32[1,16,32,512]{3,2,0,1:T(8,128)} %convert_add_fusion), calls=%async_computation | async-start | bytes 2097152 | tf_op jit(solution)/shard_map/all_to_all | solution.py:62
  142.2 501.4 %all-gather.2.cloned.1.call-start = ((), (), s32[]{:S(2)}) async-start(), calls=%async_computation.1 | async-start | bytes 17825792 | tf_op jit(solution)/shard_map/all_gather | solution.py:70
  144.2 1.0 copy-start.1
Sparse Core Ops, SparseCore 0:
  290.0 353.6 all-gather.1
where the time goes:
time: 682 us; the launch traced here: 673 us
  waiting for transfers between devices  350 us (51%)
  other arithmetic  136 us (20%)
  blocking collectives  73.1 us (11%)
  local copies, waits for them, and re-layouts  52.5 us (8%)
  matrix products  34.1 us (5%)
  between operations  17.9 us (3%)
  starting transfers between devices  10.2 us (1%)
    all_gather x1, waiting for transfers between devices, on_device(): lax.all_gather(panel_share, 'col', axis=1, tiled=True)  350 us
    another operation x15, other arithmetic, on_device(): factor = jnp.linalg.cholesky(diag)  79.4 us
    psum x1, blocking collectives, on_device(): pivot = lax.psum(picked, 'row')  73.1 us
    another operation x4, other arithmetic, right_solve(): lax.linalg.triangular_solve(factor, rows, left_side=False, lower=True, tr...  40.3 us
    gather x1, local copies, waits for them, and re-layouts, on_device(): located = jnp.take(coords, mine, axis=1)  29.9 us
    dot_general x1, matrix products, on_device(): jnp.einsum('wb,lsb->lws', far_factor, lax.all_gather(panel_share, 'col',...  22.3 us
  transfers between devices with their start and end apart: 2, of which 1 were waited for; matrix products, arithmetic and copies ran while one was open for 21% of the time, Pallas kernels for 0%

commit v1 on v0

v1 whole, which is shorter than its diff:
```python
import functools
import math

import jax
import jax.numpy as jnp
from jax import lax
from jax.experimental import pallas as pl
from jax.experimental.pallas import tpu as pltpu
from jax.sharding import PartitionSpec as P

B = 512
LB = 16
OWNED = LB * B
LANES = 128
ROOT_THREE = math.sqrt(3.0)
LENGTH = 0.05
NUGGET = 1.0
F32 = jnp.float32
BF16 = jnp.bfloat16


def matern(row_x, row_y, col_x, col_y):
    diff_x = row_x - col_x
    diff_y = row_y - col_y
    square = diff_x * diff_x + diff_y * diff_y
    scaled = (ROOT_THREE / LENGTH) * square * lax.rsqrt(jnp.maximum(square, 1e-30))
    return (1.0 + scaled) * jnp.exp(-scaled)


def split2(value):
    high = value.astype(BF16)
    return high, (value - high.astype(F32)).astype(BF16)


def dot3(a, b, dims):
    a_high, a_low = split2(a)
    b_high, b_low = split2(b)
    product = functools.partial(
        lax.dot_general, dimension_numbers=(dims, ((), ())), preferred_element_type=F32
    )
    return product(a_high, b_high) + (product(a_high, b_low) + product(a_low, b_high))


def locate_kernel(panel_ref, order_ref, coords_ref, out_ref, index_ref, table_ref, found_ref, sem):
    here = lax.axis_index("row")
    rows = OWNED // LANES
    copy = pltpu.make_async_copy(order_ref.at[pl.ds(here * rows, rows), :], index_ref, sem)
    copy.start()
    for high in range(rows):
        at = slice(high * LANES, (high + 1) * LANES)
        table_ref[high : high + 1, :LANES] = coords_ref[0:1, at]
        table_ref[high : high + 1, LANES:] = coords_ref[1:2, at]
    table = table_ref[...]
    first = table.astype(BF16)
    rest = table - first.astype(F32)
    second = rest.astype(BF16)
    third = (rest - second.astype(F32)).astype(BF16)
    pieces = jnp.concatenate([first, second, third], axis=0)
    copy.wait()
    high_iota = lax.broadcasted_iota(jnp.int32, (rows, B), 0)
    low_iota = lax.broadcasted_iota(jnp.int32, (LANES, B), 0)
    for block in range(LB):
        per = B // LANES
        index = jnp.concatenate(
            [index_ref[block * per + t : block * per + t + 1, :] for t in range(per)], axis=1
        )
        index = index - here * OWNED
        high = (high_iota == (index >> 7)).astype(F32).astype(BF16)
        spread = lax.dot_general(
            pieces,
            jnp.concatenate([high, high, high], axis=0),
            (((0,), (0,)), ((), ())),
            preferred_element_type=F32,
        )
        chosen = low_iota == (index & (LANES - 1))
        x = jnp.sum(jnp.where(chosen, spread[:LANES], 0.0), axis=0, keepdims=True)
        y = jnp.sum(jnp.where(chosen, spread[LANES:], 0.0), axis=0, keepdims=True)
        found_ref[block, 0:1, :] = x
        found_ref[block, 1:2, :] = y
        out_ref[block, 0:1, :] = x
        out_ref[block, 1:2, :] = y
    for ahead in range(3):
        local = jnp.clip(panel_ref[0] + ahead - here * LB, 0, LB - 1)
        pivot = found_ref[local]
        for block in range(LB):
            out_ref[block, 2 + 2 * ahead : 4 + 2 * ahead, :] = pivot


def locate(panel_index, order, coords):
    return pl.pallas_call(
        locate_kernel,
        out_shape=jax.ShapeDtypeStruct((LB, 8, B), F32),
        in_specs=[
            pl.BlockSpec(memory_space=pltpu.SMEM),
            pl.BlockSpec(memory_space=pl.ANY),
            pl.BlockSpec(memory_space=pltpu.VMEM),
        ],
        out_specs=pl.BlockSpec(memory_space=pltpu.VMEM),
        scratch_shapes=[
            pltpu.VMEM((OWNED // LANES, LANES), jnp.int32),
            pltpu.VMEM((OWNED // LANES, 2 * LANES), F32),
            pltpu.VMEM((LB, 2, B), F32),
            pltpu.SemaphoreType.DMA,
        ],
        name="locate",
    )(panel_index, order.reshape(-1, LANES), coords)


def update_kernel(
    panel_ref, own_ref, far_ref, pivot_ref, got_ref, inverse_ref, trailing_ref,
    panel_out, trailing_out, weight_ref, solved_ref, wide_ref,
):
    step = pl.program_id(0)
    here_row = lax.axis_index("row")
    here_col = lax.axis_index("col")
    block_k = panel_ref[0]
    share = solved_ref.shape[0] // LB
    span = weight_ref.shape[0]
    block = step * LB + here_row

    @pl.when(step == 0)
    def _():
        pivot = pivot_ref[...]
        pivot_x = pivot[0:1, :]
        pivot_y = pivot[1:2, :]
        columns = pivot.T
        wide_ref[0] = jnp.broadcast_to(columns[:, 0:1], (B, LANES))
        wide_ref[1] = jnp.broadcast_to(columns[:, 1:2], (B, LANES))
        inverse = inverse_ref[...]
        far = far_ref[...].T
        far_cov = matern(far[:, 0:1], far[:, 1:2], pivot_x, pivot_y)
        far_factor = dot3(far_cov, inverse, ((1,), (1,)))
        weight_ref[...] = dot3(far_factor, inverse, ((1,), (0,)))
        own = own_ref[...].T
        cov = matern(own[:, 0:1], own[:, 1:2], pivot_x, pivot_y)
        position = lax.broadcasted_iota(jnp.int32, (LB * share, B), 0)
        column = lax.broadcasted_iota(jnp.int32, (LB * share, B), 1)
        blocks = (position // share) * LB + here_row
        within = here_col * share + position % share
        cov = cov + jnp.where((blocks == block_k) & (within == column), NUGGET, 0.0)
        solved = dot3(cov, inverse, ((1,), (1,)))
        solved_ref[...] = jnp.where(blocks >= block_k, solved, 0.0)

    panel_out[0, 0] = solved_ref[pl.ds(step * share, share), :]

    @pl.when(block > block_k)
    def _():
        weight_high, weight_low = split2(weight_ref[...])
        for part in range(B // LANES):
            at = slice(part * LANES, (part + 1) * LANES)
            cov = matern(wide_ref[0], wide_ref[1], got_ref[0, 0:1, at], got_ref[0, 1:2, at])
            cov_high, cov_low = split2(cov)
            update = jnp.dot(weight_high, cov_high, preferred_element_type=F32) + (
                jnp.dot(weight_high, cov_low, preferred_element_type=F32)
                + jnp.dot(weight_low, cov_high, preferred_element_type=F32)
            )
            trailing_out[0, 0, :, at] = trailing_ref[0, 0, :, at] - update

    @pl.when(block <= block_k)
    def _():
        trailing_out[...] = trailing_ref[...]


def update(panel_index, own, far, pivot, got, inverse, trailing, share):
    span = trailing.shape[2]
    whole = lambda *shape: pl.BlockSpec(shape, lambda i: (0,) * len(shape))
    return pl.pallas_call(
        update_kernel,
        grid=(LB,),
        out_shape=(
            jax.ShapeDtypeStruct((LB, 1, share, B), F32),
            jax.ShapeDtypeStruct(trailing.shape, F32),
        ),
        in_specs=[
            pl.BlockSpec(memory_space=pltpu.SMEM),
            whole(8, LB * share),
            whole(8, span),
            whole(8, B),
            pl.BlockSpec((1, 8, B), lambda i: (i, 0, 0)),
            whole(B, B),
            pl.BlockSpec((1, 1, span, B), lambda i: (i, 0, 0, 0)),
        ],
        out_specs=(
            pl.BlockSpec((1, 1, share, B), lambda i: (i, 0, 0, 0)),
            pl.BlockSpec((1, 1, span, B), lambda i: (i, 0, 0, 0)),
        ),
        scratch_shapes=[
            pltpu.VMEM((span, B), F32),
            pltpu.VMEM((LB * share, B), F32),
            pltpu.VMEM((2, B, LANES), F32),
        ],
        compiler_params=pltpu.CompilerParams(vmem_limit_bytes=40 * 1024 * 1024),
        name="update",
    )(panel_index, own, far, pivot, got, inverse, trailing)


def on_device(coords, order, panel_index, trailing):
    columns = lax.axis_size("col")
    here_col = lax.axis_index("col")
    span = trailing.shape[2]
    share = B // columns
    block_k = panel_index[0]
    got = lax.all_to_all(locate(panel_index, order, coords), "row", 0, 0, tiled=True)

    def pivot_block(ahead):
        block = block_k + ahead
        return lax.dynamic_index_in_dim(got, block // LB, 0, keepdims=False)[
            2 + 2 * ahead : 4 + 2 * ahead
        ]

    pad = lambda pair: jnp.pad(pair, ((0, 6), (0, 0)))
    pivot = pivot_block(0)
    far = jnp.concatenate([pivot_block(1), pivot_block(2)], axis=1)
    far = lax.dynamic_slice_in_dim(far, here_col * span, span, 1)
    own = lax.dynamic_slice_in_dim(got[:, 0:2], here_col * share, share, 2)
    own = own.transpose(1, 0, 2).reshape(2, LB * share)
    diag = matern(pivot[0][:, None], pivot[1][:, None], pivot[0], pivot[1])
    diag = diag + NUGGET * jnp.eye(B, dtype=F32)
    factor = jnp.linalg.cholesky(diag)
    inverse = lax.linalg.triangular_solve(
        factor, jnp.eye(B, dtype=F32), left_side=True, lower=True
    )
    return update(panel_index, pad(own), pad(far), pad(pivot), got, inverse, trailing, share)


def solution(mesh):
    placed = (P(None, "row"), P(), P(), P(None, "row", "col", None))
    return jax.shard_map(
        on_device,
        mesh=mesh,
        in_specs=placed,
        out_specs=(P(None, "row", "col", None), P(None, "row", "col", None)),
        check_vma=False,
    )
```

time: 682 us -> 182 us (0.27); the launches traced: 673 us -> 184 us
  waiting for transfers between devices: 350 us -> 7.77 us
  blocking collectives: 73.1 us -> 0 us
  local copies, waits for them, and re-layouts: 52.5 us -> 10.9 us
  matrix products: 34.1 us -> 10.1 us
  Pallas kernels: 0 us -> 20.4 us
  other arithmetic: 136 us -> 122 us
  between operations: 17.9 us -> 4.02 us
    all_gather x1 -> x0, waiting for transfers between devices: 350 us -> none  [on_device(): lax.all_gather(panel_share, 'col', axis=1, tiled=True)]
    psum x1 -> x0, blocking collectives: 73.1 us -> none  [on_device(): pivot = lax.psum(picked, 'row')]
    gather x2 -> x0, local copies, waits for them, and re-layouts: 34.7 us -> none  [the longest x1 29.9 us: on_device(): located = jnp.take(coords, mine, axis=1)]
    dot_general x1 -> x0, matrix products: 22.3 us -> none  [on_device(): jnp.einsum('wb,lsb->lws', far_factor, lax.all_gather(panel_share, 'col',...]
    pallas_call x0 -> x2, Pallas kernels: none -> 20.4 us  [the longest x1 16.3 us: update(): pl.pallas_call(update_kernel, grid=(LB,), out_shape=(jax.ShapeDtypeStruct...]
    select_n x4 -> x0, other arithmetic: 8.6 us -> none  [the longest x2 7.46 us: on_device(): located = jnp.take(coords, mine, axis=1)]
    all_to_all x1, waiting for transfers between devices: 0.01 us -> 7.77 us  [on_device(): lax.all_to_all(locate(panel_index, order, coords), 'row', 0, 0, tiled=True)]
    another operation x15 -> x14, other arithmetic: 79.4 us -> 80.1 us  [on_device(): factor = jnp.linalg.cholesky(diag)]
  transfers between devices with their start and end apart: 2 -> 1, of which waited for: 1 -> 1; matrix products, arithmetic and copies ran while one was open for 21% -> 0% of each run, Pallas kernels for 0% -> 0%
where the time goes in v1:
time: 182 us; the launch traced here: 184 us
  other arithmetic  122 us (67%)
  Pallas kernels  20.4 us (11%)
  local copies, waits for them, and re-layouts  10.9 us (6%)
  matrix products  10.1 us (6%)
  starting transfers between devices  8.45 us (5%)
  waiting for transfers between devices  7.77 us (4%)
  between operations  4.02 us (2%)
    another operation x14, other arithmetic, on_device(): factor = jnp.linalg.cholesky(diag)  80.1 us
    another operation x4, other arithmetic, on_device(): lax.linalg.triangular_solve(factor, jnp.eye(B, dtype=F32), left_side=True...  40.3 us
    pallas_call x1, Pallas kernels, update(): pl.pallas_call(update_kernel, grid=(LB,), out_shape=(jax.ShapeDtypeStruct...  16.3 us
    another operation x12, local copies, waits for them, and re-layouts  10.5 us
    all_to_all x1, starting transfers between devices, on_device(): lax.all_to_all(locate(panel_index, order, coords), 'row', 0, 0, tiled=True)  8.45 us
    all_to_all x1, waiting for transfers between devices, on_device(): lax.all_to_all(locate(panel_index, order, coords), 'row', 0, 0, tiled=True)  7.77 us
    another operation x7, matrix products, on_device(): lax.linalg.triangular_solve(factor, jnp.eye(B, dtype=F32), left_side=True...  5.56 us
    another operation x6, matrix products, on_device(): factor = jnp.linalg.cholesky(diag)  4.54 us
  transfers between devices with their start and end apart: 1, of which 1 were waited for; matrix products, arithmetic and copies ran while one was open for 0% of the time, Pallas kernels for 0%

profile of v1, /device:TPU:1, one launch (start us, length us, event | category | flops | bytes accessed | tf_op | source)
XLA Modules:
  0.0 184.1 jit_solution(2865536869229372967)
XLA Ops:
  1.3 4.2 %locate.1 = f32[16,8,512]{2,1,0:T(8,128)} custom-call(s32[1]{0:T(128)} %copy.21.panel_ref, s32[1024,128]{1,0:T(8,128)} %bitcast.62, f32[2,8192]{1,0:T(2,128)} %coords_ref.1), custom_call_target="tpu_custom_call" | custom-call | tf_op jit(solution)/shard_map/locate/pallas_call | solution.py:90
  5.5 8.4 %all-to-all-start = ((f32[16,8,512]{2,1,0:T(8,128)}), f32[16,8,512]{2,1,0:T(8,128)S(1)}, u32[]{:S(2)}, u32[]{:S(2)}) async-start(f32[16,8,512]{2,1,0:T(8,128)} %locate.1), calls=%async_computation | async-start | bytes 524288 | tf_op jit(solution)/shard_map/all_to_all | solution.py:203
  13.9 0.8 iota_compare_fusion.1
  14.7 0.1 fusion.8
  14.8 7.8 %all-to-all-done.got_ref = f32[16,8,512]{2,1,0:T(8,128)S(1)} async-done(((f32[16,8,512]{2,1,0:T(8,128)}), f32[16,8,512]{2,1,0:T(8,128)S(1)}, u32[]{:S(2)}, u32[]{:S(2)}) %all-to-all-start) | async-done | bytes 262176 | tf_op jit(solution)/shard_map/all_to_all | solution.py:203
  22.6 1.1 add_multiply_fusion
  23.7 11.7 %cholesky.104 = f32[128,128]{1,0:T(8,128)S(1)} custom-call(f32[128,128]{1,0:T(8,128)S(1)} %cholesky.266), custom_call_target="Cholesky" | custom-call | tf_op jit(solution)/shard_map/jit(cholesky)/cholesky | solution.py:219
  35.4 0.6 select_reduce_fusion.3
  36.1 0.1 cholesky.224
  36.2 0.1 fusion.28
  36.3 0.1 dynamic-slice_bitcast_fusion
  36.4 0.1 reshape.57
  36.5 10.6 %custom-call.30 = f32[1,128,128]{1,2,0:T(8,128)S(1)} custom-call(f32[1,128,128]{2,1,0:T(8,128)} %get-tuple-element.34), custom_call_target="InvertDiagBlocksLowerTriangular" | custom-call | tf_op jit(solution)/shard_map/jit(cholesky)/cholesky | solution.py:219
  47.2 0.3 constant_dynamic-update-slice_fusion
  47.5 1.3 convolution_subtract_fusion.3
  48.8 11.7 %cholesky.217 = f32[128,128]{1,0:T(8,128)S(1)} custom-call(f32[128,128]{1,0:T(8,128)S(1)} %cholesky.270), custom_call_target="Cholesky" | custom-call | tf_op jit(solution)/shard_map/jit(cholesky)/cholesky | solution.py:219
  60.5 9.9 %custom-call.31 = f32[1,128,128]{1,2,0:T(8,128)S(1)} custom-call(f32[1,128,128]{2,1,0:T(8,128)S(1)} %get-tuple-element.31), custom_call_target="InvertDiagBlocksLowerTriangular" | custom-call | tf_op jit(solution)/shard_map/jit(cholesky)/cholesky | solution.py:219
  70.4 0.3 convolution_dynamic-update-slice_fusion
  70.7 1.3 convolution_subtract_fusion.4
  72.0 11.7 %cholesky.238 = f32[128,128]{1,0:T(8,128)S(1)} custom-call(f32[128,128]{1,0:T(8,128)S(1)} %cholesky.275), custom_call_target="Cholesky" | custom-call | tf_op jit(solution)/shard_map/jit(cholesky)/cholesky | solution.py:219
  83.7 0.7 compare_reduce_fusion.1
  84.4 9.8 %custom-call.32 = f32[1,128,128]{1,2,0:T(8,128)S(1)} custom-call(f32[1,128,128]{2,1,0:T(8,128)S(1)} %get-tuple-element.28), custom_call_target="InvertDiagBlocksLowerTriangular" | custom-call | tf_op jit(solution)/shard_map/jit(cholesky)/cholesky | solution.py:219
  94.2 0.2 convolution_dynamic-update-slice_fusion.1
  94.5 1.2 convolution_subtract_fusion.5
  95.7 11.9 %cholesky.255 = f32[128,128]{1,0:T(8,128)S(1)} custom-call(f32[128,128]{1,0:T(8,128)S(1)} %convolution_subtract_fusion.5), custom_call_target="Cholesky" | custom-call | tf_op jit(solution)/shard_map/jit(cholesky)/cholesky | solution.py:219
  107.6 0.7 compare_reduce_fusion
  108.3 0.6 compare_reduce_fusion.2
  111.3 0.1 select_select_fusion
  111.5 10.5 %while.1 = (s32[]{:T(128)}, f32[512,512]{1,0:T(8,128)S(1)}, s32[4,2]{0,1:T(2,128)S(1)}, f32[4,128,128]{2,1,0:T(8,128)}, s32[]{:T(128)}) while((s32[]{:T(128)}, f32[512,512]{1,0:T(8,128)S(1)}, s32[4,2]{0,1:T(2,128)S(1)}, f32[4,128,128]{2,1,0:T(8,128)}, s32[]{:T(128)}) %tuple.32), condition=%wide.while_cond, body=%wide.while_body.sunk | while | flops 2 | bytes 132205 | solution.py:220
  111.5 0.1 constant_dynamic-slice_fusion.4
  111.6 0.6 fusion.38
  112.2 2.0 %bitcast_dynamic-update-slice_fusion.2 = f32[4,128,128]{2,1,0:T(8,128)} fusion(f32[4,128,128]{2,1,0:T(8,128)} %get-tuple-element.76, s32[]{:T(128)S(6)} %copy.16, f32[512,512]{1,0:T(8,128)S(1)} %get-tuple-element.79, s32[]{:T(128)} %bitcast.54, s32[]{:T(128)} %bitcast.55), kind=kLoop, calls=%fused_computation.clone.1 | loop fusion | bytes 132100 | tf_op jit(solution)/shard_map/triangular_solve
  114.1 0.1 constant_dynamic-slice_fusion.4
  114.2 0.6 fusion.38
  114.8 2.0 %bitcast_dynamic-update-slice_fusion.2 = f32[4,128,128]{2,1,0:T(8,128)} fusion(f32[4,128,128]{2,1,0:T(8,128)} %get-tuple-element.76, s32[]{:T(128)S(6)} %copy.16, f32[512,512]{1,0:T(8,128)S(1)} %get-tuple-element.79, s32[]{:T(128)} %bitcast.54, s32[]{:T(128)} %bitcast.55), kind=kLoop, calls=%fused_computation.clone.1 | loop fusion | bytes 132100 | tf_op jit(solution)/shard_map/triangular_solve
  116.8 0.6 fusion.38
  117.4 2.0 %bitcast_dynamic-update-slice_fusion.2 = f32[4,128,128]{2,1,0:T(8,128)} fusion(f32[4,128,128]{2,1,0:T(8,128)} %get-tuple-element.76, s32[]{:T(128)S(6)} %copy.16, f32[512,512]{1,0:T(8,128)S(1)} %get-tuple-element.79, s32[]{:T(128)} %bitcast.54, s32[]{:T(128)} %bitcast.55), kind=kLoop, calls=%fused_computation.clone.1 | loop fusion | bytes 132100 | tf_op jit(solution)/shard_map/triangular_solve
  119.5 0.6 fusion.38
  120.0 2.0 %bitcast_dynamic-update-slice_fusion.2 = f32[4,128,128]{2,1,0:T(8,128)} fusion(f32[4,128,128]{2,1,0:T(8,128)} %get-tuple-element.76, s32[]{:T(128)S(6)} %copy.16, f32[512,512]{1,0:T(8,128)S(1)} %get-tuple-element.79, s32[]{:T(128)} %bitcast.54, s32[]{:T(128)} %bitcast.55), kind=kLoop, calls=%fused_computation.clone.1 | loop fusion | bytes 132100 | tf_op jit(solution)/shard_map/triangular_solve
  122.0 40.1 %custom-call.33 = f32[4,128,128]{1,2,0:T(8,128)S(1)} custom-call(f32[4,128,128]{2,1,0:T(8,128)} %get-tuple-element.9), custom_call_target="InvertDiagBlocksLowerTriangular" | custom-call | tf_op jit(solution)/shard_map/triangular_solve | solution.py:220
  162.2 1.2 fusion.10
  163.4 0.4 convolution_subtract_fusion.1
  163.7 0.4 fusion.22
  164.2 0.4 convolution_subtract_fusion
  164.6 1.3 fusion.20
  165.9 0.6 convolution_subtract_fusion.2
  166.5 1.3 fusion.19
  167.9 16.3 %update.1 = (f32[16,1,32,512]{3,2,1,0:T(8,128)}, f32[16,1,64,512]{3,2,1,0:T(8,128)}) custom-call(s32[1]{0:T(128)} %copy.21.panel_ref, f32[8,512]{1,0:T(8,128)S(1)} %pad.12.own_ref, f32[8,64]{1,0:T(8,128)S(1)} %pad.13.far_ref, f32[8,512]{1,0:T(8,128)S(1)} %pad.14.pivot_ref, f32[16,8,512]{2,1,0:T(8,128)S(1)} %all-to-all-done.got_ref, ...), custom_call_target="tpu_custom_call" | custom-call | tf_op jit(solution)/shard_map/update/pallas_call | solution.py:167
  (25 shorter events, 0.4 us)
Async XLA Ops:
  5.5 17.1 %all-to-all-start = ((f32[16,8,512]{2,1,0:T(8,128)}), f32[16,8,512]{2,1,0:T(8,128)S(1)}, u32[]{:S(2)}, u32[]{:S(2)}) async-start(f32[16,8,512]{2,1,0:T(8,128)} %locate.1), calls=%async_computation | async-start | bytes 524288 | tf_op jit(solution)/shard_map/all_to_all | solution.py:203
  23.7 23.8 %copy-start.1 = (f32[512,512]{1,0:T(8,128)}, f32[512,512]{1,0:T(8,128)S(1)}, u32[]{:S(2)}) copy-start(f32[512,512]{1,0:T(8,128)S(1)} %add_multiply_fusion) | copy-start | bytes 3145732
  162.2 1.6 copy-start.2
  165.9 2.0 %copy-start = (f32[16,1,64,512]{3,2,1,0:T(8,128)S(1)}, f32[16,1,64,512]{3,2,1,0:T(8,128)}, u32[]{:S(2)}) copy-start(f32[16,1,64,512]{3,2,1,0:T(8,128)} %trailing_ref.1) | copy-start | bytes 6291460

commit v2 on v1

--- a/solution.py
+++ b/solution.py
@@ -106,9 +106,127 @@
     )(panel_index, order.reshape(-1, LANES), coords)
 
 
+TILE = 8
+CORE = 64
+
+
+def column_of(value, at):
+    return jnp.broadcast_to(value[:, at : at + 1], (TILE, LANES))
+
+
+def row_of(value, at):
+    return jnp.broadcast_to(value[at : at + 1, :], (TILE, LANES))
+
+
+def inverse_factor(rows):
+    rows = list(rows)
+    count = len(rows)
+    sub = lax.broadcasted_iota(jnp.int32, (TILE, LANES), 0)
+    lane = lax.broadcasted_iota(jnp.int32, (TILE, LANES), 1)
+    others = [(sub != i).astype(F32) for i in range(TILE)]
+    below = [(sub > i).astype(F32) for i in range(TILE)]
+
+    def columns(row, panel):
+        return [column_of(rows[row], TILE * panel + c) for c in range(TILE)]
+
+    ahead = columns(0, 0)
+    for j in range(count):
+        last = j == count - 1
+        inside = (lane >= TILE * j) & (lane < TILE * (j + 1))
+        left = [columns(i, j) for i in range(j + 1, count)]
+        here = list(ahead)
+        if not last:
+            next_left = list(left[0])
+            ahead = columns(j + 1, j + 1)
+        lower = jnp.where(inside, (lane - TILE * j == sub).astype(F32), rows[j])
+        both = lower
+        scale = jnp.ones((TILE, LANES), F32)
+        for i in range(TILE):
+            inverse_pivot = 1.0 / row_of(here[i], i)
+            by_others = here[i] * (inverse_pivot * others[i])
+            by_below = here[i] * (inverse_pivot * below[i])
+            if not last:
+                by_next = next_left[i] * inverse_pivot
+            for c in range(i + 1, TILE):
+                pivot_row = row_of(here[c], i)
+                here[c] = here[c] - by_others * pivot_row
+                if not last:
+                    next_left[c] = next_left[c] - by_next * pivot_row
+            if not last:
+                for c in range(TILE):
+                    ahead[c] = ahead[c] - by_next * row_of(next_left[i], c)
+            lower = lower - by_below * row_of(lower, i)
+            both = both - by_others * row_of(both, i)
+            scale = jnp.where(sub == i, inverse_pivot, scale)
+        rows[j] = lower * lax.rsqrt(1.0 / scale)
+        if last:
+            break
+        both = both * scale
+        spread = [row_of(both, c) for c in range(TILE)]
+        for i in range(j + 1, count):
+            terms = [left[i - j - 1][c] * spread[c] for c in range(TILE)]
+            while len(terms) > 1:
+                terms = [terms[t] + terms[t + 1] for t in range(0, len(terms), 2)]
+            rows[i] = jnp.where(inside, 0.0, rows[i]) - terms[0]
+    return rows
+
+
+def split3(value):
+    first = value.astype(BF16)
+    rest = value - first.astype(F32)
+    second = rest.astype(BF16)
+    return first, second, (rest - second.astype(F32)).astype(BF16)
+
+
+def dot6(a, b, dims):
+    a1, a2, a3 = split3(a)
+    b1, b2, b3 = split3(b)
+    left, right = dims
+    return lax.dot_general(
+        jnp.concatenate([a1, a2, a1, a2, a1, a3], axis=left),
+        jnp.concatenate([b1, b1, b2, b2, b3, b1], axis=right),
+        (((left,), (right,)), ((), ())),
+        preferred_element_type=F32,
+    )
+
+
+def factor_in_place(matrix):
+    order = matrix.shape[0]
+    for start in range(0, order, CORE):
+        base = start // LANES * LANES
+        half = start - base
+        block = matrix[start : start + CORE, base : base + LANES]
+        if half:
+            block = pltpu.roll(block, LANES - half, 1)
+        core = jnp.concatenate(
+            inverse_factor([block[t : t + TILE] for t in range(0, CORE, TILE)]), axis=0
+        )[:, :CORE]
+        sub = lax.broadcasted_iota(jnp.int32, (CORE, CORE), 0)
+        lane = lax.broadcasted_iota(jnp.int32, (CORE, CORE), 1)
+        core = jnp.where(sub >= lane, core, 0.0)
+        zero = jnp.zeros((CORE, CORE), F32)
+        placed = jnp.concatenate([zero, core] if half else [core, zero], axis=1)
+        rest = order - start - CORE
+        if rest:
+            below = matrix[start + CORE :, base : base + LANES]
+            factor = dot6(below, placed, (1, 1))
+        solved = dot6(core, matrix[start : start + CORE, :], (1, 0))
+        lane = lax.broadcasted_iota(jnp.int32, (CORE, LANES), 1)
+        inside = (lane >= half) & (lane < half + CORE)
+        parts = [solved[:, at : at + LANES] for at in range(0, order, LANES)]
+        parts[base // LANES] = jnp.where(inside, placed, parts[base // LANES])
+        solved = jnp.concatenate(parts, axis=1)
+        matrix[start : start + CORE, :] = solved
+        if rest:
+            lane = lax.broadcasted_iota(jnp.int32, (rest, LANES), 1)
+            inside = (lane >= half) & (lane < half + CORE)
+            matrix[start + CORE :, base : base + LANES] = jnp.where(inside, 0.0, below)
+            matrix[start + CORE :, :] = matrix[start + CORE :, :] - dot6(factor, solved, (1, 0))
+
+
 def update_kernel(
-    panel_ref, own_ref, far_ref, pivot_ref, got_ref, inverse_ref, trailing_ref,
-    panel_out, trailing_out, weight_ref, solved_ref, wide_ref,
+    panel_ref, got_ref, trailing_ref,
+    panel_out, trailing_out, weight_ref, solved_ref, wide_ref, matrix_ref, turned_ref,
 ):
     step = pl.program_id(0)
     here_row = lax.axis_index("row")
@@ -120,19 +238,41 @@
 
     @pl.when(step == 0)
     def _():
-        pivot = pivot_ref[...]
-        pivot_x = pivot[0:1, :]
-        pivot_y = pivot[1:2, :]
-        columns = pivot.T
-        wide_ref[0] = jnp.broadcast_to(columns[:, 0:1], (B, LANES))
-        wide_ref[1] = jnp.broadcast_to(columns[:, 1:2], (B, LANES))
-        inverse = inverse_ref[...]
-        far = far_ref[...].T
-        far_cov = matern(far[:, 0:1], far[:, 1:2], pivot_x, pivot_y)
-        far_factor = dot3(far_cov, inverse, ((1,), (1,)))
+        pivot = got_ref[block_k // LB]
+        pivot_x = pivot[2:3, :]
+        pivot_y = pivot[3:4, :]
+        turned = pivot.T
+        wide_ref[0] = jnp.broadcast_to(turned[:, 2:3], (B, LANES))
+        wide_ref[1] = jnp.broadcast_to(turned[:, 3:4], (B, LANES))
+        for part in range(B // LANES):
+            at = slice(part * LANES, (part + 1) * LANES)
+            cov = matern(wide_ref[0], wide_ref[1], pivot_x[:, at], pivot_y[:, at])
+            row = lax.broadcasted_iota(jnp.int32, (B, LANES), 0)
+            lane = lax.broadcasted_iota(jnp.int32, (B, LANES), 1) + part * LANES
+            matrix_ref[:, at] = cov + jnp.where(row == lane, NUGGET, 0.0)
+        factor_in_place(matrix_ref)
+        row = lax.broadcasted_iota(jnp.int32, (B, B), 0)
+        column = lax.broadcasted_iota(jnp.int32, (B, B), 1)
+        inverse = jnp.where(row >= column, matrix_ref[...], 0.0)
+
+        spans = B // span
+        ahead = 1 + here_col // spans
+        turned_ref[:, :TILE] = got_ref[(block_k + ahead) // LB].T
+        far = turned_ref[pl.ds(here_col % spans * span, span), :TILE]
+        far_x = jnp.where(ahead == 1, far[:, 4:5], far[:, 6:7])
+        far_y = jnp.where(ahead == 1, far[:, 5:6], far[:, 7:8])
+        far_factor = dot3(matern(far_x, far_y, pivot_x, pivot_y), inverse, ((1,), (1,)))
         weight_ref[...] = dot3(far_factor, inverse, ((1,), (0,)))
-        own = own_ref[...].T
-        cov = matern(own[:, 0:1], own[:, 1:2], pivot_x, pivot_y)
+
+        turned_ref[...] = got_ref[...].reshape(LB * TILE, B).T
+        own = turned_ref[pl.ds(here_col * share, share), :]
+        cov = jnp.concatenate(
+            [
+                matern(own[:, t : t + 1], own[:, t + 1 : t + 2], pivot_x, pivot_y)
+                for t in range(0, LB * TILE, TILE)
+            ],
+            axis=0,
+        )
         position = lax.broadcasted_iota(jnp.int32, (LB * share, B), 0)
         column = lax.broadcasted_iota(jnp.int32, (LB * share, B), 1)
         blocks = (position // share) * LB + here_row
@@ -148,11 +288,12 @@
         weight_high, weight_low = split2(weight_ref[...])
         for part in range(B // LANES):
             at = slice(part * LANES, (part + 1) * LANES)
-            cov = matern(wide_ref[0], wide_ref[1], got_ref[0, 0:1, at], got_ref[0, 1:2, at])
-            cov_high, cov_low = split2(cov)
-            update = jnp.dot(weight_high, cov_high, preferred_element_type=F32) + (
-                jnp.dot(weight_high, cov_low, preferred_element_type=F32)
-                + jnp.dot(weight_low, cov_high, preferred_element_type=F32)
+            x = got_ref[step, 0:1, at]
+            y = got_ref[step, 1:2, at]
+            cov_high, cov_low = split2(matern(wide_ref[0], wide_ref[1], x, y))
+            product = functools.partial(jnp.dot, preferred_element_type=F32)
+            update = product(weight_high, cov_high) + (
+                product(weight_high, cov_low) + product(weight_low, cov_high)
             )
             trailing_out[0, 0, :, at] = trailing_ref[0, 0, :, at] - update
 
@@ -161,9 +302,8 @@
         trailing_out[...] = trailing_ref[...]
 
 
-def update(panel_index, own, far, pivot, got, inverse, trailing, share):
+def update(panel_index, got, trailing, share):
     span = trailing.shape[2]
-    whole = lambda *shape: pl.BlockSpec(shape, lambda i: (0,) * len(shape))
     return pl.pallas_call(
         update_kernel,
         grid=(LB,),
@@ -173,11 +313,7 @@
         ),
         in_specs=[
             pl.BlockSpec(memory_space=pltpu.SMEM),
-            whole(8, LB * share),
-            whole(8, span),
-            whole(8, B),
-            pl.BlockSpec((1, 8, B), lambda i: (i, 0, 0)),
-            whole(B, B),
+            pl.BlockSpec(got.shape, lambda i: (0, 0, 0)),
             pl.BlockSpec((1, 1, span, B), lambda i: (i, 0, 0, 0)),
         ],
         out_specs=(
@@ -188,39 +324,18 @@
             pltpu.VMEM((span, B), F32),
             pltpu.VMEM((LB * share, B), F32),
             pltpu.VMEM((2, B, LANES), F32),
+            pltpu.VMEM((B, B), F32),
+            pltpu.VMEM((B, LANES), F32),
         ],
-        compiler_params=pltpu.CompilerParams(vmem_limit_bytes=40 * 1024 * 1024),
+        compiler_params=pltpu.CompilerParams(vmem_limit_bytes=48 * 1024 * 1024),
         name="update",
-    )(panel_index, own, far, pivot, got, inverse, trailing)
+    )(panel_index, got, trailing)
 
 
 def on_device(coords, order, panel_index, trailing):
-    columns = lax.axis_size("col")
-    here_col = lax.axis_index("col")
-    span = trailing.shape[2]
-    share = B // columns
-    block_k = panel_index[0]
+    share = B // lax.axis_size("col")
     got = lax.all_to_all(locate(panel_index, order, coords), "row", 0, 0, tiled=True)
-
-    def pivot_block(ahead):
-        block = block_k + ahead
-        return lax.dynamic_index_in_dim(got, block // LB, 0, keepdims=False)[
-            2 + 2 * ahead : 4 + 2 * ahead
-        ]
-
-    pad = lambda pair: jnp.pad(pair, ((0, 6), (0, 0)))
-    pivot = pivot_block(0)
-    far = jnp.concatenate([pivot_block(1), pivot_block(2)], axis=1)
-    far = lax.dynamic_slice_in_dim(far, here_col * span, span, 1)
-    own = lax.dynamic_slice_in_dim(got[:, 0:2], here_col * share, share, 2)
-    own = own.transpose(1, 0, 2).reshape(2, LB * share)
-    diag = matern(pivot[0][:, None], pivot[1][:, None], pivot[0], pivot[1])
-    diag = diag + NUGGET * jnp.eye(B, dtype=F32)
-    factor = jnp.linalg.cholesky(diag)
-    inverse = lax.linalg.triangular_solve(
-        factor, jnp.eye(B, dtype=F32), left_side=True, lower=True
-    )
-    return update(panel_index, pad(own), pad(far), pad(pivot), got, inverse, trailing, share)
+    return update(panel_index, got, trailing, share)
 
 
 def solution(mesh):

time: 182 us -> 53 us (0.29); the launches traced: 184 us -> 52.1 us
  other arithmetic: 122 us -> 0 us
  blocking collectives: 0 us -> 17.1 us
  Pallas kernels: 20.4 us -> 32.1 us
  matrix products: 10.1 us -> 0 us
  local copies, waits for them, and re-layouts: 10.9 us -> 1.59 us
  starting transfers between devices: 8.45 us -> 0 us
  waiting for transfers between devices: 7.77 us -> 0 us
  between operations: 4.02 us -> 1.29 us
    another operation x18 -> x0, other arithmetic: 120 us -> none  [the longest x14 80.1 us: on_device(): factor = jnp.linalg.cholesky(diag)]
    all_to_all x0 -> x1, blocking collectives: none -> 17.1 us  [on_device(): lax.all_to_all(locate(panel_index, order, coords), 'row', 0, 0, tiled=True)]
    pallas_call x1, Pallas kernels: 16.3 us -> 27.9 us  [update(): pl.pallas_call(update_kernel, grid=(LB,), out_shape=(jax.ShapeDtypeStruct...]
    another operation x17 -> x0, local copies, waits for them, and re-layouts: 10.7 us -> none
    another operation x13 -> x0, matrix products: 10.1 us -> none  [the longest x7 5.56 us: on_device(): lax.linalg.triangular_solve(factor, jnp.eye(B, dtype=F32), left_side=True...]
    all_to_all x1 -> x0, starting transfers between devices: 8.45 us -> none  [on_device(): lax.all_to_all(locate(panel_index, order, coords), 'row', 0, 0, tiled=True)]
    all_to_all x1 -> x0, waiting for transfers between devices: 7.77 us -> none  [on_device(): lax.all_to_all(locate(panel_index, order, coords), 'row', 0, 0, tiled=True)]
  transfers between devices with their start and end apart: 1 -> 0, of which waited for: 1 -> 0; matrix products, arithmetic and copies ran while one was open for 0% -> 0% of each run, Pallas kernels for 0% -> 0%
where the time goes in v2:
time: 53 us; the launch traced here: 52.1 us
  Pallas kernels  32.1 us (61%)
  blocking collectives  17.1 us (32%)
  local copies, waits for them, and re-layouts  1.59 us (3%)
  between operations  1.29 us (2%)
    pallas_call x1, Pallas kernels, update(): pl.pallas_call(update_kernel, grid=(LB,), out_shape=(jax.ShapeDtypeStruct...  27.9 us
    all_to_all x1, blocking collectives, on_device(): lax.all_to_all(locate(panel_index, order, coords), 'row', 0, 0, tiled=True)  17.1 us
    pallas_call x1, Pallas kernels, locate(): pl.pallas_call(locate_kernel, out_shape=jax.ShapeDtypeStruct((LB, 8, B),...  4.17 us
    unnamed x2, local copies, waits for them, and re-layouts  1.59 us

profile of v2, /device:TPU:1, one launch (start us, length us, event | category | flops | bytes accessed | tf_op | source)
XLA Modules:
  0.0 52.1 jit_solution(3509987998841905853)
XLA Ops:
  1.3 4.2 %locate.1 = f32[16,8,512]{2,1,0:T(8,128)} custom-call(s32[1]{0:T(128)S(6)} %copy.6.panel_ref, s32[1024,128]{1,0:T(8,128)} %bitcast.1, f32[2,8192]{1,0:T(2,128)} %coords_ref.1), custom_call_target="tpu_custom_call" | custom-call | tf_op jit(solution)/shard_map/locate/pallas_call | solution.py:90
  5.4 17.1 %all_to_all.5.got_ref = f32[16,8,512]{2,1,0:T(8,128)S(1)} all-to-all(f32[16,8,512]{2,1,0:T(8,128)} %locate.1), channel_id=1, replica_groups=mesh['row'=16,'col'=16] {'row'}, dimensions={0} | all-to-all | bytes 524288 | tf_op jit(solution)/shard_map/all_to_all | solution.py:337
  22.6 0.0 copy-start
  22.6 1.6 %copy-done = f32[16,1,64,512]{3,2,1,0:T(8,128)S(1)} copy-done((f32[16,1,64,512]{3,2,1,0:T(8,128)S(1)}, f32[16,1,64,512]{3,2,1,0:T(8,128)}, u32[]{:S(2)}) %copy-start) | copy-done | bytes 2097176
  24.2 27.9 %update.1 = (f32[16,1,32,512]{3,2,1,0:T(8,128)}, f32[16,1,64,512]{3,2,1,0:T(8,128)}) custom-call(s32[1]{0:T(128)S(6)} %copy.6.panel_ref, f32[16,8,512]{2,1,0:T(8,128)S(1)} %all_to_all.5.got_ref, f32[16,1,64,512]{3,2,1,0:T(8,128)S(1)} %copy-done), custom_call_target="tpu_custom_call" | custom-call | tf_op jit(solution)/shard_map/update/pallas_call | solution.py:307
Async XLA Ops:
  22.6 1.6 %copy-start = (f32[16,1,64,512]{3,2,1,0:T(8,128)S(1)}, f32[16,1,64,512]{3,2,1,0:T(8,128)}, u32[]{:S(2)}) copy-start(f32[16,1,64,512]{3,2,1,0:T(8,128)} %trailing_ref.1) | copy-start | bytes 6291460
